TPU v7x, 32 devices: a whole 2x2x4 slice. The times are simulated.
32 devices in a mesh: ha: 8 (over y, x, core), wa: 4 (over z).
Axes of the slice: x: 2, y: 2, z: 4, core: 2. Of those that a mesh axis runs over, the one named last changes fastest.
Arguments:
- frames: bfloat16 [2, 128, 256, 384], P(None, 'ha', 'wa'), may hold values from -6 to 6
- keep: int32 [2, 3], replicated, may hold values 0 or 1
- expand_weight: bfloat16 [384, 1536], replicated, may hold values from -0.3125 to 0.3125
- dw_kernel: float32 [3, 3, 1536], replicated, may hold values from -2 to 2
- conv_bias: float32 [1536], replicated, may hold values from -3 to 3
- project_weight: bfloat16 [1536, 384], replicated, may hold values from -0.15625 to 0.15625
- qkv_weight: bfloat16 [384, 1152], replicated, may hold values from -4 to 4
- out_weight: bfloat16 [384, 384], replicated, may hold values from -0.3125 to 0.3125
- mlp_in: bfloat16 [384, 1536], replicated, may hold values from -0.3125 to 0.3125
- mlp_out: bfloat16 [1536, 384], replicated, may hold values from -0.15625 to 0.15625
Outputs:
- result: bfloat16 [2, 128, 256, 384], P(None, 'ha', 'wa')
All inputs are finite; a program needn't handle non-finite values.
Results may differ from a plain program's by a relative error of at most 0.0068.
Values may be sent and summed in bfloat16 or wider, within the bound.
No kernel may reach another device: no remote copies, remote signals or barrier semaphores. Data moves between devices by JAX's collectives and lax.ppermute only.
A program may use at most 64 MiB of HBM per device.

v0:
```python
import jax
import jax.numpy as jnp
from jax import lax
from jax.sharding import PartitionSpec as P

HEADS = 12
GRID = 16


def with_halo(x, sides, width):
    for axis, dim in sides:
        size, length = (lax.axis_size(axis), x.shape[dim])
        up = [(i, (i + 1) % size) for i in range(size - 1)]
        down = [(j, i) for i, j in up]
        last = lax.slice_in_dim(x, length - width, length, axis=dim)
        initial = lax.slice_in_dim(x, 0, width, axis=dim)
        before = lax.ppermute(last, axis, up)
        after = lax.ppermute(initial, axis, down)
        x = jnp.concatenate([before, x, after], axis=dim)
    return x


def normalize(values):
    mean_val = jnp.mean(values, axis=-1, keepdims=True)
    centred = values - mean_val
    variance = jnp.mean(centred * centred, axis=-1, keepdims=True)
    return centred * lax.rsqrt(variance + 1e-05)


def attend(block, window_flag, qkv_weight, out_weight):
    pair_count, token_count, channels = block.shape
    head_dim = channels // HEADS
    residual = block.astype(jnp.float32)
    normed = normalize(residual).astype(jnp.bfloat16)
    qkv = jnp.dot(normed, qkv_weight, preferred_element_type=jnp.float32).astype(jnp.bfloat16)
    queries = qkv[..., :channels].reshape(pair_count, token_count, HEADS, head_dim)
    keys_part = qkv[..., channels : 2 * channels].reshape(pair_count, token_count, HEADS, head_dim)
    values_part = qkv[..., 2 * channels :].reshape(pair_count, token_count, HEADS, head_dim)
    scores = jnp.einsum(
        "bqhd,bkhd->bhqk", queries, keys_part, preferred_element_type=jnp.float32
    ) * head_dim ** (-0.5)
    top_score = jnp.max(scores, axis=-1, keepdims=True)
    weights = jnp.exp(scores - top_score)
    probs = (weights / jnp.sum(weights, axis=-1, keepdims=True)).astype(jnp.bfloat16)
    attended = jnp.einsum("bhqk,bkhd->bqhd", probs, values_part, preferred_element_type=jnp.float32)
    attended = attended.astype(jnp.bfloat16).reshape(pair_count, token_count, channels)
    update = jnp.dot(attended, out_weight, preferred_element_type=jnp.float32)
    return (residual + window_flag[:, None, None] * update).astype(jnp.bfloat16)


def body(
    frames,
    keep,
    expand_weight,
    dw_kernel,
    conv_bias,
    project_weight,
    qkv_weight,
    out_weight,
    mlp_in,
    mlp_out,
):
    frame_count, row_count, col_count, channels = frames.shape
    rows_axis = lax.axis_size("ha")
    cols_axis = lax.axis_size("wa")
    flags = keep.astype(jnp.float32)
    framed = with_halo(frames, (("ha", 1), ("wa", 2)), 1)
    padded = jax.nn.gelu(jnp.dot(framed, expand_weight, preferred_element_type=jnp.float32)).astype(
        jnp.bfloat16
    )
    total = jnp.zeros((frame_count, row_count, col_count, padded.shape[-1]), jnp.float32)
    for shift_y in range(3):
        for shift_x in range(3):
            total = (
                total
                + padded[:, shift_y : shift_y + row_count, shift_x : shift_x + col_count, :].astype(
                    jnp.float32
                )
                * dw_kernel[shift_y, shift_x]
            )
    mixed = jax.nn.gelu(total + conv_bias).astype(jnp.bfloat16)
    branch = jnp.dot(mixed, project_weight, preferred_element_type=jnp.float32)
    first = (frames.astype(jnp.float32) + flags[:, 0][:, None, None, None] * branch).astype(
        jnp.bfloat16
    )
    row_stride = row_count * rows_axis // GRID
    col_stride = col_count * cols_axis // GRID
    rows_each = row_stride // rows_axis
    cols_each = col_stride // cols_axis
    row_groups = row_count // row_stride
    col_groups = col_count // col_stride
    outgoing = first.reshape(
        frame_count, row_groups, rows_axis, rows_each, col_groups, cols_axis, cols_each, channels
    )
    outgoing = outgoing.transpose(0, 2, 5, 3, 6, 1, 4, 7)
    flat_send = outgoing.reshape(
        frame_count, rows_axis * cols_axis, rows_each, cols_each, row_groups, col_groups, channels
    )
    arrived = lax.all_to_all(flat_send, ("ha", "wa"), split_axis=1, concat_axis=1, tiled=True)
    arrived = arrived.reshape(
        frame_count, rows_axis, cols_axis, rows_each, cols_each, row_groups, col_groups, channels
    )
    windows = arrived.transpose(0, 3, 4, 1, 5, 2, 6, 7).reshape(-1, GRID * GRID, channels)
    window_count = windows.shape[0]
    window_flags = jnp.repeat(flags[:, 1], window_count // frame_count).reshape(
        window_count // 2, 2
    )
    blocks = windows.reshape(window_count // 2, 2, GRID * GRID, channels)

    def one_pair(pair):
        return attend(pair[0], pair[1], qkv_weight, out_weight)

    second = lax.map(one_pair, (blocks, window_flags))
    second = second.reshape(
        frame_count, rows_each, cols_each, rows_axis, row_groups, cols_axis, col_groups, channels
    )
    second = second.transpose(0, 3, 5, 1, 2, 4, 6, 7)
    flat_back = second.reshape(
        frame_count, rows_axis * cols_axis, rows_each, cols_each, row_groups, col_groups, channels
    )
    returned = lax.all_to_all(flat_back, ("ha", "wa"), split_axis=1, concat_axis=1, tiled=True)
    returned = returned.reshape(
        frame_count, rows_axis, cols_axis, rows_each, cols_each, row_groups, col_groups, channels
    )
    restored = returned.transpose(0, 5, 1, 3, 6, 2, 4, 7).reshape(
        frame_count, row_count, col_count, channels
    )
    residual = restored.astype(jnp.float32)
    normed = normalize(residual).astype(jnp.bfloat16)
    inner = jax.nn.gelu(jnp.dot(normed, mlp_in, preferred_element_type=jnp.float32)).astype(
        jnp.bfloat16
    )
    update = jnp.dot(inner, mlp_out, preferred_element_type=jnp.float32)
    return (residual + flags[:, 2][:, None, None, None] * update).astype(jnp.bfloat16)


def solution(mesh):
    in_specs = (P(None, "ha", "wa", None), P(), P(), P(), P(), P(), P(), P(), P(), P())
    out_specs = P(None, "ha", "wa", None)
    return jax.shard_map(body, mesh=mesh, in_specs=in_specs, out_specs=out_specs, check_vma=False)
```

profile of v0, /device:TPU:1, one launch (start us, length us, event | category | flops | bytes accessed | tf_op | source)
XLA Modules:
  0.0 231.1 jit_solution(10826536203100216102)
XLA Ops:
  0.0 1.1 fusion.82
  1.1 4.5 %collective-permute-start = (bf16[2,1,64,384]{3,2,1,0:T(8,128)(2,1)S(1)}, bf16[2,1,64,384]{3,2,1,0:T(8,128)(2,1)S(1)}, u32[]{:S(2)}, u32[]{:S(2)}) collective-permute-start(bf16[2,1,64,384]{3,2,1,0:T(8,128)(2,1)S(1)} %get-tuple-element.70), channel_id=1, source_target_pairs={{0,4},{4,8},{8,12},{12,16},{16,20},{20,24},{24,28},{1,5},{5,9},{9,... | collective-permute-start | bytes 294920 | tf_op jit(solution)/shard_map/ppermute | solution.py:17
  5.6 1.9 collective-permute-start.1
  7.5 0.7 convert_element_type.94
  8.2 1.1 slice_reduce_fusion.8
  9.3 1.7 constant_dynamic-update-slice_fusion.1
  11.0 0.5 collective-permute-done.1
  11.6 3.2 %collective-permute-start.2 = (bf16[2,18,1,384]{3,2,1,0:T(2,128)(2,1)S(1)}, bf16[2,18,1,384]{3,2,1,0:T(2,128)(2,1)S(1)}, u32[]{:S(2)}, u32[]{:S(2)}) collective-permute-start(bf16[2,18,1,384]{3,2,1,0:T(2,128)(2,1)S(1)} %get-tuple-element.67), channel_id=1, source_target_pairs={{0,1},{1,2},{2,3},{4,5},{5,6},{6,7},{8,9},{9,10},{10,11},{12,13},{... | collective-permute-start | bytes 82952 | tf_op jit(solution)/shard_map/ppermute | solution.py:17
  14.8 1.3 collective-permute-start.3
  16.1 0.2 slice_reduce_fusion.9
  16.4 3.3 %collective-permute-done.3 = bf16[2,18,1,384]{3,2,1,0:T(2,128)(2,1)S(1)} collective-permute-done((bf16[2,18,1,384]{3,2,1,0:T(2,128)(2,1)S(1)}, bf16[2,18,1,384]{3,2,1,0:T(2,128)(2,1)S(1)}, u32[]{:S(2)}, u32[]{:S(2)}) %collective-permute-start.3) | collective-permute-done | bytes 27680 | tf_op jit(solution)/shard_map/ppermute | solution.py:18
  19.8 6.9 %fusion.34 = bf16[2,18,66,1536]{3,2,1,0:T(8,128)(2,1)S(1)} fusion(bf16[2,18,1,384]{3,2,1,0:T(2,128)(2,1)S(1)} %collective-permute-done.3, bf16[2,18,64,384]{3,2,1,0:T(8,128)(2,1)S(1)} %constant_dynamic-update-slice_fusion, bf16[2,18,1,384]{3,2,1,0:T(2,128)(2,1)S(1)} %collective-permute-done.2, bf16[384,1536]{1,0:T(8,128)(2,1)S(1)} %copy-done), kind=kOutput, calls=%fused_computation.43 | convolution fusion | flops 2841163776 | bytes 10303488 | tf_op jit(solution)/shard_map/dot_general | solution.py:68
  26.7 19.0 %add_convert_fusion.1 = bf16[2,16,64,384]{3,2,1,0:T(8,128)(2,1)} fusion(bf16[2,16,64,384]{3,2,1,0:T(8,128)(2,1)S(1)} %copy-done.4, bf16[2,18,66,1536]{3,2,1,0:T(8,128)(2,1)S(1)} %fusion.34, f32[1536]{0:T(1024)S(1)} %copy-done.8, f32[1536]{0:T(1024)S(1)} %get-tuple-element.45, f32[1536]{0:T(1024)S(1)} %get-tuple-element.46, f32[1536]{0:T(1024)S(1)} %get-tuple-element.39, ...), kind=kOutput, calls=%fused_computation.64 | convolution fusion | flops 2532311040 | bytes 61030912 | tf_op jit(solution)/shard_map/dot_general | solution.py:82
  45.7 2.9 %reshape.94 = bf16[2,2,8,1,4,4,4,384]{7,6,5,4,2,1,0,3:T(4,128)(2,1)S(1)} reshape(bf16[2,16,64,384]{3,2,1,0:T(8,128)(2,1)} %add_convert_fusion.1) | data formatting | bytes 3145728 | tf_op jit(solution)/shard_map/reshape | solution.py:92
  48.6 0.7 copy.61
  49.4 2.0 copy.62
  51.4 6.2 %all-to-all-start = ((bf16[2,32,1,4,2,4,384]{6,5,4,3,0,2,1:T(4,128)(2,1)}), bf16[2,32,1,4,2,4,384]{6,5,4,3,0,2,1:T(4,128)(2,1)S(1)}, u32[]{:S(2)}, u32[]{:S(2)}) async-start(bf16[2,32,1,4,2,4,384]{6,5,4,3,0,2,1:T(4,128)(2,1)} %copy.62), calls=%async_computation | async-start | bytes 3145728 | tf_op jit(solution)/shard_map/all_to_all | solution.py:99
  57.7 37.2 %all-to-all-done = bf16[2,32,1,4,2,4,384]{6,5,4,3,0,2,1:T(4,128)(2,1)S(1)} async-done(((bf16[2,32,1,4,2,4,384]{6,5,4,3,0,2,1:T(4,128)(2,1)}), bf16[2,32,1,4,2,4,384]{6,5,4,3,0,2,1:T(4,128)(2,1)S(1)}, u32[]{:S(2)}, u32[]{:S(2)}) %all-to-all-start) | async-done | bytes 1572896 | tf_op jit(solution)/shard_map/all_to_all | solution.py:99
  94.9 0.5 copy.63
  95.5 1.8 copy.64
  97.2 2.7 %reshape_reshape.4 = bf16[4,2,256,384]{3,2,1,0:T(8,128)(2,1)S(1)} reshape(bf16[2,1,4,8,2,4,4,384]{7,6,5,4,3,2,0,1:T(4,128)(2,1)} %copy.64) | data formatting | bytes 3145728 | tf_op jit(solution)/shard_map/reshape;reshape | solution.py:108
  100.1 54.2 %while.10 = (s32[]{:T(128)}, bf16[4,2,256,384]{3,2,1,0:T(8,128)(2,1)}, bf16[4,2,256,384]{3,2,1,0:T(8,128)(2,1)S(1)}, f32[4,2]{1,0:T(4,128)S(1)}, bf16[384,1152]{...) while((s32[]{:T(128)}, bf16[4,2,256,384]{3,2,1,0:T(8,128)(2,1)}, ...), condition=%wide.region_5.6_spmd, body=%wide.region_0.5_spmd.sunk | while | flops 816710400 | bytes 36244140 | solution.py:113
  100.2 0.3 fusion.109
  100.5 0.7 copy-done.2
  101.2 2.0 convolution_convert_fusion.2
  103.4 0.2 copy.88
  103.6 0.2 copy.89
  103.8 4.9 %fusion.111 = (f32[2,12,256]{2,1,0:T(8,128)S(1)}, f32[2,12,256,256]{2,3,1,0:T(8,128)}) fusion(bf16[2,256,12,32]{1,3,2,0:T(8,128)(2,1)S(1)} %bitcast.117, bf16[2,256,12,32]{1,3,2,0:T(8,128)(2,1)S(1)} %bitcast.118), kind=kOutput, calls=%fused_computation.105.clone.1 | convolution fusion | flops 105382144 | bytes 7102464 | tf_op jit(solution)/shard_map/while/body/eval_jaxpr/sub | solution.py:43
  108.8 3.6 %fusion.112 = bf16[2,12,32,256]{3,2,1,0:T(8,128)(2,1)S(1)} fusion(bf16[2,256,12,32]{1,3,2,0:T(8,128)(2,1)S(1)} %bitcast.119, f32[2,12,256,256]{2,3,1,0:T(8,128)} %get-tuple-element.116, f32[2,12,256]{2,1,0:T(8,128)S(1)} %get-tuple-element.117), kind=kOutput, calls=%fused_computation.11.clone.1 | convolution fusion | flops 104005632 | bytes 7102464 | tf_op jit(solution)/shard_map/while/body/eval_jaxpr/bhqk,bkhd->bqhd/dot_general | solution.py:45
  112.4 1.2 fusion.114
  113.8 0.3 fusion.109
  114.1 0.7 copy-done.2
  114.8 2.0 convolution_convert_fusion.2
  116.9 0.2 copy.88
  117.3 4.9 %fusion.111 = (f32[2,12,256]{2,1,0:T(8,128)S(1)}, f32[2,12,256,256]{2,3,1,0:T(8,128)}) fusion(bf16[2,256,12,32]{1,3,2,0:T(8,128)(2,1)S(1)} %bitcast.117, bf16[2,256,12,32]{1,3,2,0:T(8,128)(2,1)S(1)} %bitcast.118), kind=kOutput, calls=%fused_computation.105.clone.1 | convolution fusion | flops 105382144 | bytes 7102464 | tf_op jit(solution)/shard_map/while/body/eval_jaxpr/sub | solution.py:43
  122.4 3.6 %fusion.112 = bf16[2,12,32,256]{3,2,1,0:T(8,128)(2,1)S(1)} fusion(bf16[2,256,12,32]{1,3,2,0:T(8,128)(2,1)S(1)} %bitcast.119, f32[2,12,256,256]{2,3,1,0:T(8,128)} %get-tuple-element.116, f32[2,12,256]{2,1,0:T(8,128)S(1)} %get-tuple-element.117), kind=kOutput, calls=%fused_computation.11.clone.1 | convolution fusion | flops 104005632 | bytes 7102464 | tf_op jit(solution)/shard_map/while/body/eval_jaxpr/bhqk,bkhd->bqhd/dot_general | solution.py:45
  126.0 1.2 fusion.114
  127.3 0.3 fusion.109
  127.6 0.7 copy-done.2
  128.3 2.0 convolution_convert_fusion.2
  130.9 4.9 %fusion.111 = (f32[2,12,256]{2,1,0:T(8,128)S(1)}, f32[2,12,256,256]{2,3,1,0:T(8,128)}) fusion(bf16[2,256,12,32]{1,3,2,0:T(8,128)(2,1)S(1)} %bitcast.117, bf16[2,256,12,32]{1,3,2,0:T(8,128)(2,1)S(1)} %bitcast.118), kind=kOutput, calls=%fused_computation.105.clone.1 | convolution fusion | flops 105382144 | bytes 7102464 | tf_op jit(solution)/shard_map/while/body/eval_jaxpr/sub | solution.py:43
  135.9 3.6 %fusion.112 = bf16[2,12,32,256]{3,2,1,0:T(8,128)(2,1)S(1)} fusion(bf16[2,256,12,32]{1,3,2,0:T(8,128)(2,1)S(1)} %bitcast.119, f32[2,12,256,256]{2,3,1,0:T(8,128)} %get-tuple-element.116, f32[2,12,256]{2,1,0:T(8,128)S(1)} %get-tuple-element.117), kind=kOutput, calls=%fused_computation.11.clone.1 | convolution fusion | flops 104005632 | bytes 7102464 | tf_op jit(solution)/shard_map/while/body/eval_jaxpr/bhqk,bkhd->bqhd/dot_general | solution.py:45
  139.5 1.2 fusion.114
  140.9 0.3 fusion.109
  141.2 0.7 copy-done.2
  141.9 2.0 convolution_convert_fusion.2
  144.1 0.2 copy.88
  144.4 4.9 %fusion.111 = (f32[2,12,256]{2,1,0:T(8,128)S(1)}, f32[2,12,256,256]{2,3,1,0:T(8,128)}) fusion(bf16[2,256,12,32]{1,3,2,0:T(8,128)(2,1)S(1)} %bitcast.117, bf16[2,256,12,32]{1,3,2,0:T(8,128)(2,1)S(1)} %bitcast.118), kind=kOutput, calls=%fused_computation.105.clone.1 | convolution fusion | flops 105382144 | bytes 7102464 | tf_op jit(solution)/shard_map/while/body/eval_jaxpr/sub | solution.py:43
  149.5 3.6 %fusion.112 = bf16[2,12,32,256]{3,2,1,0:T(8,128)(2,1)S(1)} fusion(bf16[2,256,12,32]{1,3,2,0:T(8,128)(2,1)S(1)} %bitcast.119, f32[2,12,256,256]{2,3,1,0:T(8,128)} %get-tuple-element.116, f32[2,12,256]{2,1,0:T(8,128)S(1)} %get-tuple-element.117), kind=kOutput, calls=%fused_computation.11.clone.1 | convolution fusion | flops 104005632 | bytes 7102464 | tf_op jit(solution)/shard_map/while/body/eval_jaxpr/bhqk,bkhd->bqhd/dot_general | solution.py:45
  153.1 1.2 fusion.114
  154.3 2.9 %reshape.97 = bf16[2,1,4,8,2,4,4,384]{7,6,5,4,3,2,0,1:T(4,128)(2,1)S(1)} reshape(bf16[4,2,256,384]{3,2,1,0:T(8,128)(2,1)} %get-tuple-element.37) | data formatting | bytes 3145728 | tf_op jit(solution)/shard_map/reshape | solution.py:114
  157.2 0.7 copy.65
  157.9 0.8 copy.66
  158.8 40.7 %all_to_all.10 = bf16[2,32,1,4,2,4,384]{6,5,4,3,0,2,1:T(4,128)(2,1)S(1)} all-to-all(bf16[2,32,1,4,2,4,384]{6,5,4,3,0,2,1:T(4,128)(2,1)S(1)} %copy.66), channel_id=1, replica_groups=mesh['ha'=8,'wa'=4] {'ha','wa'}, dimensions={1} | all-to-all | bytes 3145728 | tf_op jit(solution)/shard_map/all_to_all | solution.py:121
  199.5 0.9 copy_convert_fusion
  200.4 3.7 %copy.68 = f32[2,32,1,4,2,4,384]{6,5,4,3,1,0,2:T(4,128)} copy(f32[2,32,1,4,2,4,384]{6,1,5,4,3,2,0:T(8,128)S(1)} %copy_convert_fusion) | data formatting | bytes 6291456 | tf_op jit(solution)/shard_map/convert_element_type | solution.py:128
  204.1 2.7 %reduce_sum.45 = f32[2,2,8,4,4,4]{3,1,5,4,2,0:T(2,128)S(1)} reduce(f32[2,2,8,1,4,4,4,384]{7,4,1,6,5,2,0,3:T(4,128)} %bitcast.114, f32[]{:T(128)} %constant.31.clone.1), dimensions={3,7}, to_apply=%region_6.7 | reduce | flops 784384 | bytes 3153924 | tf_op jit(solution)/shard_map/reduce_sum | solution.py:24
  206.8 0.5 copy.70
  207.3 0.5 copy.73
  208.0 4.6 %copy.69 = f32[2,2,8,1,4,4,4,384]{7,6,5,4,2,1,0,3:T(4,128)} copy(f32[2,2,8,1,4,4,4,384]{7,4,1,6,5,2,0,3:T(4,128)} %bitcast.115) | data formatting | bytes 6291456 | tf_op jit(solution)/shard_map/convert_element_type | solution.py:128
  212.6 1.5 multiply_reduce_fusion.1
  214.1 0.5 copy.74
  215.2 5.0 %reshape.99 = f32[2,16,64,384]{3,2,1,0:T(8,128)} reshape(f32[2,2,8,1,4,4,4,384]{7,6,5,4,2,1,0,3:T(4,128)} %copy.69) | data formatting | bytes 6291456 | tf_op jit(solution)/shard_map/convert_element_type | solution.py:128
  220.2 10.9 %add_convert_fusion = bf16[2,16,64,384]{3,2,1,0:T(8,128)(2,1)} fusion(f32[2,16,64,384]{3,2,1,0:T(8,128)} %reshape.99, f32[2,16,64]{2,1,0:T(8,128)S(1)} %copy.76, f32[2,16,64]{2,1,0:T(8,128)S(1)} %copy.72, f32[2]{0:T(128)S(1)} %get-tuple-element.47, bf16[1536,384]{1,0:T(8,128)(2,1)S(1)} %copy-done.6, bf16[384,1536]{1,0:T(8,128)(2,1)} %param.20), kind=kOutput, calls=%fused_computation.61 | convolution fusion | flops 4864868352 | bytes 7094280 | tf_op jit(solution)/shard_map/dot_general | solution.py:133
  (71 shorter events, 3.7 us)
Async XLA Ops:
  0.0 19.7 %copy-start = (bf16[384,1536]{1,0:T(8,128)(2,1)S(1)}, bf16[384,1536]{1,0:T(8,128)(2,1)}, u32[]{:S(2)}) copy-start(bf16[384,1536]{1,0:T(8,128)(2,1)} %param.14) | copy-start | bytes 3538948
  1.1 8.2 %collective-permute-start = (bf16[2,1,64,384]{3,2,1,0:T(8,128)(2,1)S(1)}, bf16[2,1,64,384]{3,2,1,0:T(8,128)(2,1)S(1)}, u32[]{:S(2)}, u32[]{:S(2)}) collective-permute-start(bf16[2,1,64,384]{3,2,1,0:T(8,128)(2,1)S(1)} %get-tuple-element.70), channel_id=1, source_target_pairs={{0,4},{4,8},{8,12},{12,16},{16,20},{20,24},{24,28},{1,5},{5,9},{9,... | collective-permute-start | bytes 294920 | tf_op jit(solution)/shard_map/ppermute | solution.py:17
  5.6 5.9 %collective-permute-start.1 = (bf16[2,1,64,384]{3,2,1,0:T(8,128)(2,1)S(1)}, bf16[2,1,64,384]{3,2,1,0:T(8,128)(2,1)S(1)}, u32[]{:S(2)}, u32[]{:S(2)}) collective-permute-start(bf16[2,1,64,384]{3,2,1,0:T(8,128)(2,1)S(1)} %get-tuple-element.69), channel_id=1, source_target_pairs={{4,0},{8,4},{12,8},{16,12},{20,16},{24,20},{28,24},{5,1},{9,5},{13... | collective-permute-start | bytes 294920 | tf_op jit(solution)/shard_map/ppermute | solution.py:18
  11.6 4.8 %collective-permute-start.2 = (bf16[2,18,1,384]{3,2,1,0:T(2,128)(2,1)S(1)}, bf16[2,18,1,384]{3,2,1,0:T(2,128)(2,1)S(1)}, u32[]{:S(2)}, u32[]{:S(2)}) collective-permute-start(bf16[2,18,1,384]{3,2,1,0:T(2,128)(2,1)S(1)} %get-tuple-element.67), channel_id=1, source_target_pairs={{0,1},{1,2},{2,3},{4,5},{5,6},{6,7},{8,9},{9,10},{10,11},{12,13},{... | collective-permute-start | bytes 82952 | tf_op jit(solution)/shard_map/ppermute | solution.py:17
  14.8 4.9 %collective-permute-start.3 = (bf16[2,18,1,384]{3,2,1,0:T(2,128)(2,1)S(1)}, bf16[2,18,1,384]{3,2,1,0:T(2,128)(2,1)S(1)}, u32[]{:S(2)}, u32[]{:S(2)}) collective-permute-start(bf16[2,18,1,384]{3,2,1,0:T(2,128)(2,1)S(1)} %get-tuple-element.68), channel_id=1, source_target_pairs={{1,0},{2,1},{3,2},{5,4},{6,5},{7,6},{9,8},{10,9},{11,10},{13,12},{... | collective-permute-start | bytes 82952 | tf_op jit(solution)/shard_map/ppermute | solution.py:18
  16.4 10.3 %copy-start.4 = (bf16[2,16,64,384]{3,2,1,0:T(8,128)(2,1)S(1)}, bf16[2,16,64,384]{3,2,1,0:T(8,128)(2,1)}, u32[]{:S(2)}) copy-start(bf16[2,16,64,384]{3,2,1,0:T(8,128)(2,1)} %param.12) | copy-start | bytes 4718596
  16.4 10.3 %copy-start.5 = (bf16[1536,384]{1,0:T(8,128)(2,1)S(1)}, bf16[1536,384]{1,0:T(8,128)(2,1)}, u32[]{:S(2)}) copy-start(bf16[1536,384]{1,0:T(8,128)(2,1)} %param.17) | copy-start | bytes 3538948
  16.4 10.3 %copy-start.8 = (f32[1536]{0:T(1024)S(1)}, f32[1536]{0:T(1024)}, u32[]{:S(2)}) copy-start(f32[1536]{0:T(1024)} %param.16) | copy-start | bytes 18436
  51.4 48.7 %copy-start.7 = (bf16[384,384]{1,0:T(8,128)(2,1)S(1)}, bf16[384,384]{1,0:T(8,128)(2,1)}, u32[]{:S(2)}) copy-start(bf16[384,384]{1,0:T(8,128)(2,1)} %param.19) | copy-start | bytes 884740
  51.4 43.5 %all-to-all-start = ((bf16[2,32,1,4,2,4,384]{6,5,4,3,0,2,1:T(4,128)(2,1)}), bf16[2,32,1,4,2,4,384]{6,5,4,3,0,2,1:T(4,128)(2,1)S(1)}, u32[]{:S(2)}, u32[]{:S(2)}) async-start(bf16[2,32,1,4,2,4,384]{6,5,4,3,0,2,1:T(4,128)(2,1)} %copy.62), calls=%async_computation | async-start | bytes 3145728 | tf_op jit(solution)/shard_map/all_to_all | solution.py:99
  100.1 1.1 copy-start.2
  108.8 3.6 %copy-start.3 = (bf16[4,2,256,384]{3,2,1,0:T(8,128)(2,1)S(1)}, bf16[4,2,256,384]{3,2,1,0:T(8,128)(2,1)}, u32[]{:S(2)}) copy-start(bf16[4,2,256,384]{3,2,1,0:T(8,128)(2,1)} %copy-done.2) | copy-start | bytes 4718596 | tf_op jit(solution)/shard_map/while
  113.6 1.1 copy-start.2
  122.4 3.6 %copy-start.3 = (bf16[4,2,256,384]{3,2,1,0:T(8,128)(2,1)S(1)}, bf16[4,2,256,384]{3,2,1,0:T(8,128)(2,1)}, u32[]{:S(2)}) copy-start(bf16[4,2,256,384]{3,2,1,0:T(8,128)(2,1)} %copy-done.2) | copy-start | bytes 4718596 | tf_op jit(solution)/shard_map/while
  127.2 1.1 copy-start.2
  135.9 3.6 %copy-start.3 = (bf16[4,2,256,384]{3,2,1,0:T(8,128)(2,1)S(1)}, bf16[4,2,256,384]{3,2,1,0:T(8,128)(2,1)}, u32[]{:S(2)}) copy-start(bf16[4,2,256,384]{3,2,1,0:T(8,128)(2,1)} %copy-done.2) | copy-start | bytes 4718596 | tf_op jit(solution)/shard_map/while
  140.7 1.1 copy-start.2
  149.5 3.6 %copy-start.3 = (bf16[4,2,256,384]{3,2,1,0:T(8,128)(2,1)S(1)}, bf16[4,2,256,384]{3,2,1,0:T(8,128)(2,1)}, u32[]{:S(2)}) copy-start(bf16[4,2,256,384]{3,2,1,0:T(8,128)(2,1)} %copy-done.2) | copy-start | bytes 4718596 | tf_op jit(solution)/shard_map/while
  207.9 4.7 %copy-start.1 = (f32[2,32,1,4,2,4,384]{6,5,4,3,1,0,2:T(4,128)S(1)}, f32[2,32,1,4,2,4,384]{6,5,4,3,1,0,2:T(4,128)}, u32[]{:S(2)}) copy-start(f32[2,32,1,4,2,4,384]{6,5,4,3,1,0,2:T(4,128)} %copy.68) | copy-start | bytes 9437188
  212.6 7.6 %copy-start.6 = (bf16[1536,384]{1,0:T(8,128)(2,1)S(1)}, bf16[1536,384]{1,0:T(8,128)(2,1)}, u32[]{:S(2)}) copy-start(bf16[1536,384]{1,0:T(8,128)(2,1)} %param.21) | copy-start | bytes 3538948
where the time goes:
time: 232 us; the launch traced here: 231 us
  matrix products  83.6 us (36%)
  waiting for transfers between devices  41 us (18%)
  blocking collectives  40.7 us (18%)
  local copies, waits for them, and re-layouts  40.5 us (17%)
  starting transfers between devices  17.1 us (7%)
  other arithmetic  7.59 us (3%)
    all_to_all x1, blocking collectives, body(): lax.all_to_all(flat_back, ('ha', 'wa'), split_axis=1, concat_axis=1, tile...  40.7 us
    all_to_all x1, waiting for transfers between devices, body(): lax.all_to_all(flat_send, ('ha', 'wa'), split_axis=1, concat_axis=1, tile...  37.2 us
    sub x4, matrix products, attend(): weights = jnp.exp(scores - top_score)  19.5 us
    dot_general x1, matrix products, body(): branch = jnp.dot(mixed, project_weight, preferred_element_type=jnp.float32)  19 us
    dot_general x4, matrix products, attend(): jnp.einsum('bhqk,bkhd->bqhd', probs, values_part, preferred_element_type=...  14.3 us
    convert_element_type x3, local copies, waits for them, and re-layouts, body(): residual = restored.astype(jnp.float32)  13.3 us
    dot_general x1, matrix products, body(): update = jnp.dot(inner, mlp_out, preferred_element_type=jnp.float32)  10.9 us
    dot_general x4, matrix products, attend(): jnp.dot(normed, qkv_weight, preferred_element_type=jnp.float32)  8.15 us
  transfers between devices with their start and end apart: 5, of which 3 were waited for; matrix products, arithmetic and copies ran while one was open for 2% of the time, Pallas kernels for 0%

commit v1 on v0

v1 whole, which is shorter than its diff:
```python
import math

import jax
import jax.numpy as jnp
import numpy as np
from jax import lax
from jax.experimental import pallas as pl
from jax.experimental.pallas import tpu as pltpu
from jax.sharding import PartitionSpec as P

HEADS = 12
GRID = 16
SEG = 8
CHUNK = 256
F32 = jnp.float32
BF16 = jnp.bfloat16
VMEM_LIMIT = 40 * 1024 * 1024


def gelu(v):
    cubic = v * (math.sqrt(2 / math.pi) + (math.sqrt(2 / math.pi) * 0.044715) * (v * v))
    half = 0.5 * v
    return half + half * jnp.tanh(cubic)


def normalize(values):
    mean_val = jnp.mean(values, axis=-1, keepdims=True)
    centred = values - mean_val
    variance = jnp.mean(centred * centred, axis=-1, keepdims=True)
    return centred * lax.rsqrt(variance + 1e-05)


def dot(a, b):
    return jnp.dot(a, b, preferred_element_type=F32)


def dot_t(a, b):
    return lax.dot_general(a, b, (((1,), (1,)), ((), ())), preferred_element_type=F32)


def segment_order(cols, count):
    steps = cols // SEG
    matrix = np.zeros((count * cols, count * cols), np.float32)
    for row in range(count):
        for t in range(steps):
            for s in range(SEG):
                matrix[row * cols + t * SEG + s, row * cols + s * steps + t] = 1
    return matrix


def message_order(row_groups, cols, col_stride, cols_each):
    col_groups = cols // col_stride
    dests = col_stride // cols_each
    matrix = np.zeros((row_groups * cols, row_groups * cols), np.float32)
    place = 0
    for w in range(dests):
        for b in range(cols_each):
            for g in range(row_groups):
                for h in range(col_groups):
                    matrix[place, g * cols + h * col_stride + w * cols_each + b] = 1
                    place += 1
    return matrix


def conv_kernel(
    frame,
    keep_ref,
    x_ref,
    top_ref,
    bottom_ref,
    left_ref,
    right_ref,
    seg_ref,
    order_ref,
    expand_ref,
    dw_ref,
    bias_ref,
    project_ref,
    out_ref,
    tokens,
    sides,
    side_vals,
    expanded,
    mixed,
    total,
):
    step = pl.program_id(0)
    rows, cols, channels = x_ref.shape
    steps = cols // SEG
    width = expand_ref.shape[1]

    @pl.when(step == 0)
    def _():
        pair = 2 * cols
        seg_pair = seg_ref[...]
        seg_one = seg_pair[:cols, :cols]
        tokens[0:cols] = dot(seg_one, top_ref[0:cols]).astype(BF16)
        for r in range(rows // 2):
            both = x_ref[2 * r : 2 * r + 2].reshape(pair, channels)
            tokens[cols + r * pair : cols + (r + 1) * pair] = dot(seg_pair, both).astype(BF16)
        tokens[(rows + 1) * cols : (rows + 2) * cols] = dot(seg_one, bottom_ref[0:cols]).astype(BF16)
        sides[...] = jnp.zeros_like(sides)
        top = top_ref[cols : cols + 16].astype(F32)
        bottom = bottom_ref[cols : cols + 16].astype(F32)
        sides[0:1] = top[0:1]
        sides[1 : rows + 1] = left_ref[...].astype(F32)
        sides[rows + 1 : rows + 2] = bottom[0:1]
        sides[24:25] = top[1:2]
        sides[25 : rows + 25] = right_ref[...].astype(F32)
        sides[rows + 25 : rows + 26] = bottom[1:2]

    weight = expand_ref[...]
    block = 3
    for rb in range((rows + 2) // block):
        piece = tokens[rb * block * cols : (rb + 1) * block * cols]
        value = gelu(dot(piece, weight))
        expanded[rb * block : (rb + 1) * block, 1 : steps + 1] = value.reshape(block, steps, SEG, width)
    side_vals[...] = gelu(dot(sides[...].astype(BF16), weight))
    place = lax.broadcasted_iota(jnp.int32, (SEG, width), 0)
    for r in range(rows + 2):
        before = pltpu.roll(expanded[r, steps], 1, 0)
        expanded[r, 0] = jnp.where(place == 0, side_vals[r : r + 1], before)
        after = pltpu.roll(expanded[r, 1], SEG - 1, 0)
        expanded[r, steps + 1] = jnp.where(place == SEG - 1, side_vals[24 + r : 25 + r], after)

    for lt in range(width // 128):
        lanes = slice(lt * 128, (lt + 1) * 128)
        taps = [[dw_ref[3 * i + j : 3 * i + j + 1, lanes].reshape(1, 1, 128) for j in range(3)] for i in range(3)]
        shift = bias_ref[0:1, lanes].reshape(1, 1, 128)

        def one_row(r, _):
            acc = jnp.broadcast_to(shift, (steps, SEG, 128))
            for i in range(3):
                window = expanded[r + i, :, :, lanes]
                for j in range(3):
                    acc = acc + window[j : j + steps] * taps[i][j]
            value = gelu(acc).reshape(cols, 128).astype(BF16)
            mixed[pl.ds(pl.multiple_of(r * cols, cols), cols), lanes] = value
            return 0

        lax.fori_loop(0, rows, one_row, 0, unroll=2)

    branch = dot(mixed[...], project_ref[...])

    @pl.when(step == 0)
    def _():
        total[...] = branch

    @pl.when(step > 0)
    def _():
        total[...] += branch

    @pl.when(step == pl.num_programs(0) - 1)
    def _():
        flag = keep_ref[frame, 0].astype(F32)
        span = order_ref.shape[0]
        groups = span // cols
        stride = rows // groups
        order = order_ref[...]
        for d in range(stride):
            parts = []
            for g in range(groups):
                r = g * stride + d
                residual = tokens[(r + 1) * cols : (r + 2) * cols].astype(F32)
                parts.append((residual + flag * total[r * cols : (r + 1) * cols]).astype(BF16))
            value = parts[0] if groups == 1 else jnp.concatenate(parts, axis=0)
            out_ref[d * span : (d + 1) * span] = dot(order, value).astype(BF16)


def conv_call(frame, keep, x, top, bottom, left, right, seg, order, expand_weight, dw, bias, project_weight):
    rows, cols, channels = x.shape
    hidden = expand_weight.shape[1]
    steps = cols // SEG
    span = order.shape[0]

    def whole(a):
        return pl.BlockSpec(a.shape, lambda e, n=a.ndim: (0,) * n)

    def body(*refs):
        conv_kernel(frame, *refs)

    return pl.pallas_call(
        body,
        grid=(hidden // CHUNK,),
        in_specs=[
            pl.BlockSpec(memory_space=pltpu.SMEM),
            whole(x),
            whole(top),
            whole(bottom),
            whole(left),
            whole(right),
            whole(seg),
            whole(order),
            pl.BlockSpec((channels, CHUNK), lambda e: (0, e)),
            pl.BlockSpec((9, CHUNK), lambda e: (0, e)),
            pl.BlockSpec((1, CHUNK), lambda e: (0, e)),
            pl.BlockSpec((CHUNK, channels), lambda e: (e, 0)),
        ],
        out_specs=pl.BlockSpec((rows * cols, channels), lambda e: (0, 0)),
        out_shape=jax.ShapeDtypeStruct((rows * cols, channels), BF16),
        scratch_shapes=[
            pltpu.VMEM(((rows + 2) * cols, channels), BF16),
            pltpu.VMEM((48, channels), F32),
            pltpu.VMEM((48, CHUNK), F32),
            pltpu.VMEM((rows + 2, steps + 2, SEG, CHUNK), F32),
            pltpu.VMEM((rows * cols, CHUNK), BF16),
            pltpu.VMEM((rows * cols, channels), F32),
        ],
        compiler_params=pltpu.CompilerParams(vmem_limit_bytes=VMEM_LIMIT),
        cost_estimate=pl.CostEstimate(flops=6 * 10**9, bytes_accessed=4 * 10**6, transcendentals=4 * 10**6),
    )(keep, x, top, bottom, left, right, seg, order, expand_weight, dw, bias, project_weight)


def attend_kernel(frame, keep_ref, x_ref, query_ref, key_ref, value_ref, out_w_ref, out_ref, held):
    windows = held.shape[1]
    sources, _, group, channels = held.shape
    count = sources * group
    head_dim = channels // HEADS
    per_tile = 128 // head_dim
    scale = head_dim ** (-0.5) * math.log2(math.e)
    held[...] = x_ref[...].astype(F32).reshape(held.shape)
    flag = keep_ref[frame, 1].astype(F32)

    def one_window(w, _):
        residual = held[:, w].reshape(count, channels)
        normed = normalize(residual).astype(BF16)
        queries = dot_t(query_ref[...], normed).astype(BF16)
        keys_part = dot(normed, key_ref[...]).astype(BF16)
        values_part = dot_t(value_ref[...], normed).astype(BF16)
        outs = []
        for h in range(HEADS):
            tile, inside = h // per_tile, h % per_tile
            query = queries[h * head_dim : (h + 1) * head_dim]
            pieces = []
            if inside > 0:
                pieces.append(jnp.zeros((inside * head_dim, count), BF16))
            pieces.append(query)
            if inside < per_tile - 1:
                pieces.append(jnp.zeros(((per_tile - 1 - inside) * head_dim, count), BF16))
            padded = jnp.concatenate(pieces, axis=0)
            scores = dot(keys_part[:, tile * 128 : (tile + 1) * 128], padded)
            top_score = jnp.max(scores, axis=0, keepdims=True)
            weights = jnp.exp2((scores - top_score) * scale)
            norm = jnp.sum(weights, axis=0, keepdims=True)
            value = values_part[h * head_dim : (h + 1) * head_dim]
            outs.append(dot(value, weights.astype(BF16)) * (1.0 / norm))
        attended = jnp.concatenate(outs, axis=0).T.astype(BF16)
        update = dot(attended, out_w_ref[...])
        held[:, w] = (residual + flag * update).reshape(sources, group, channels)
        return 0

    lax.fori_loop(0, windows, one_window, 0)
    out_ref[...] = held[...].reshape(out_ref.shape).astype(BF16)


def attend_call(frame, keep, x, windows, group, query_w, key_w, value_w, out_weight):
    tokens, channels = x.shape
    held = (tokens // (windows * group), windows, group, channels)

    def body(*refs):
        attend_kernel(frame, *refs)

    return pl.pallas_call(
        body,
        in_specs=[pl.BlockSpec(memory_space=pltpu.SMEM)] + [pl.BlockSpec(memory_space=pltpu.VMEM)] * 5,
        out_specs=pl.BlockSpec(memory_space=pltpu.VMEM),
        out_shape=jax.ShapeDtypeStruct(x.shape, BF16),
        scratch_shapes=[pltpu.VMEM(held, F32)],
        compiler_params=pltpu.CompilerParams(vmem_limit_bytes=VMEM_LIMIT),
        cost_estimate=pl.CostEstimate(flops=6 * 10**9, bytes_accessed=3 * 10**6, transcendentals=4 * 10**6),
    )(keep, x, query_w, key_w, value_w, out_weight)


def mlp_kernel(frame, keep_ref, x_ref, order_ref, in_ref, outw_ref, *rest):
    out_ref = rest[-1]
    _, rows, cols, channels = out_ref.shape
    span = order_ref.shape[0]
    groups = span // cols
    stride = rows // groups
    flag = keep_ref[frame, 2].astype(F32)
    order = order_ref[...]
    for d in range(stride):
        residual = x_ref[d * span : (d + 1) * span].astype(F32)
        normed = normalize(residual).astype(BF16)
        inner = gelu(dot(normed, in_ref[...])).astype(BF16)
        value = (residual + flag * dot(inner, outw_ref[...])).astype(BF16)
        back = dot(order, value).astype(BF16)
        for g in range(groups):
            out_ref[0, g * stride + d] = back[g * cols : (g + 1) * cols]


def mlp_call(frame, keep, x, order, mlp_in, mlp_out, out_shape, previous):
    _, rows, cols, channels = out_shape

    def whole(a):
        return pl.BlockSpec(a.shape, lambda i, n=a.ndim: (0,) * n)

    def body(*refs):
        mlp_kernel(frame, *refs)

    args = [keep, x, order, mlp_in, mlp_out]
    specs = [pl.BlockSpec(memory_space=pltpu.SMEM)] + [whole(a) for a in args[1:]]
    aliases = {}
    if previous is not None:
        aliases = {len(args): 0}
        args.append(previous)
        specs.append(pl.BlockSpec(memory_space=pl.ANY))
    return pl.pallas_call(
        body,
        grid=(1,),
        in_specs=specs,
        out_specs=pl.BlockSpec((1, rows, cols, channels), lambda i: (frame, 0, 0, 0)),
        out_shape=jax.ShapeDtypeStruct(out_shape, BF16),
        input_output_aliases=aliases,
        compiler_params=pltpu.CompilerParams(vmem_limit_bytes=VMEM_LIMIT),
        cost_estimate=pl.CostEstimate(flops=5 * 10**9, bytes_accessed=4 * 10**6, transcendentals=2 * 10**6),
    )(*args)


def body(
    frames,
    keep,
    expand_weight,
    dw_kernel,
    conv_bias,
    project_weight,
    qkv_weight,
    out_weight,
    mlp_in,
    mlp_out,
):
    frame_count, rows, cols, channels = frames.shape
    rows_axis = lax.axis_size("ha")
    cols_axis = lax.axis_size("wa")
    row_stride = rows * rows_axis // GRID
    col_stride = cols * cols_axis // GRID
    assert row_stride == rows_axis and col_stride % cols_axis == 0
    cols_each = col_stride // cols_axis
    row_groups = rows // row_stride
    col_groups = cols // col_stride
    group = row_groups * col_groups
    devices = rows_axis * cols_axis

    right_way = [(i, i + 1) for i in range(cols_axis - 1)]
    left_way = [(j, i) for i, j in right_way]
    left = lax.ppermute(frames[:, :, cols - 1], "wa", right_way)
    right = lax.ppermute(frames[:, :, 0], "wa", left_way)
    down_way = [(i, i + 1) for i in range(rows_axis - 1)]
    up_way = [(j, i) for i, j in down_way]

    def edge(r):
        spare = jnp.zeros((frame_count, 14, channels), BF16)
        return jnp.concatenate([frames[:, r], left[:, r : r + 1], right[:, r : r + 1], spare], axis=1)

    top = lax.ppermute(edge(rows - 1), "ha", down_way)
    bottom = lax.ppermute(edge(0), "ha", up_way)

    to_segments = segment_order(cols, 2)
    to_message = message_order(row_groups, cols, col_stride, cols_each)
    from_segments = np.kron(np.eye(row_groups), segment_order(cols, 1)).T
    seg = jnp.asarray(to_segments, BF16)
    order = jnp.asarray(to_message @ from_segments, BF16)
    order_back = jnp.asarray(to_message.T, BF16)
    dw = dw_kernel.reshape(9, -1)
    bias = conv_bias.reshape(1, -1)
    query_w = qkv_weight[:, :channels].T
    key_w = qkv_weight[:, channels : 2 * channels]
    value_w = qkv_weight[:, 2 * channels :].T

    def exchange(x):
        message = x.reshape(devices, -1, channels)
        return lax.all_to_all(message, ("ha", "wa"), split_axis=0, concat_axis=0, tiled=True).reshape(-1, channels)

    sent = []
    for f in range(frame_count):
        first = conv_call(
            f,
            keep,
            frames[f],
            top[f],
            bottom[f],
            left[f],
            right[f],
            seg,
            order,
            expand_weight,
            dw,
            bias,
            project_weight,
        )
        sent.append(exchange(first))
    back = []
    for f in range(frame_count):
        x = sent[f]
        if group == 8:
            second = attend_call(f, keep, x, cols_each, 8, query_w, key_w, value_w, out_weight)
        else:
            x = x.reshape(devices, cols_each, group, channels).swapaxes(0, 1).reshape(-1, 8, channels)
            x = x.reshape(cols_each, -1, 8, channels).swapaxes(0, 1).reshape(-1, channels)
            second = attend_call(f, keep, x, cols_each, 8, query_w, key_w, value_w, out_weight)
            second = second.reshape(-1, cols_each, 8, channels).swapaxes(0, 1)
            second = second.reshape(cols_each, devices, group, channels).swapaxes(0, 1).reshape(-1, channels)
        back.append(exchange(second))
    result = None
    for f in range(frame_count):
        result = mlp_call(f, keep, back[f], order_back, mlp_in, mlp_out, frames.shape, result)
    return result


def solution(mesh):
    in_specs = (P(None, "ha", "wa", None), P(), P(), P(), P(), P(), P(), P(), P(), P())
    out_specs = P(None, "ha", "wa", None)
    return jax.shard_map(body, mesh=mesh, in_specs=in_specs, out_specs=out_specs, check_vma=False)
```

time: 232 us -> 145 us (0.62)
  matrix products: 83.6 us -> 0 us
  Pallas kernels: 0 us -> 81 us
  blocking collectives: 40.7 us -> 0 us
  local copies, waits for them, and re-layouts: 40.5 us -> 10.7 us
  waiting for transfers between devices: 41 us -> 23.3 us
  starting transfers between devices: 17.1 us -> 28.8 us
  other arithmetic: 7.59 us -> 0.11 us
    pallas_call x0 -> x6, Pallas kernels: none -> 81 us  [the longest x2 34 us: attend_call(): pl.pallas_call(body, in_specs=[pl.BlockSpec(memory_space=pltpu.SMEM)] + [...]
    dot_general x15 -> x0, matrix products: 64.1 us -> none  [the longest x1 19 us: body(): branch = jnp.dot(mixed, project_weight, preferred_element_type=jnp.float32)]
    all_to_all x1 -> x0, blocking collectives: 40.7 us -> none  [body(): lax.all_to_all(flat_back, ('ha', 'wa'), split_axis=1, concat_axis=1, tile...]
    sub x4 -> x0, matrix products: 19.5 us -> none  [attend(): weights = jnp.exp(scores - top_score)]
    all_to_all x1 -> x4, waiting for transfers between devices: 37.2 us -> 21.5 us  [exchange(): lax.all_to_all(message, ('ha', 'wa'), split_axis=0, concat_axis=0, tiled=...]
    convert_element_type x3 -> x0, local copies, waits for them, and re-layouts: 13.3 us -> none  [body(): residual = restored.astype(jnp.float32)]
    all_to_all x1 -> x4, starting transfers between devices: 6.18 us -> 16.4 us  [exchange(): lax.all_to_all(message, ('ha', 'wa'), split_axis=0, concat_axis=0, tiled=...]
    reshape x6 -> x2, local copies, waits for them, and re-layouts: 10.1 us -> 0.04 us  [the longest x1 0.03 us: body(): dw = dw_kernel.reshape(9, -1)]
  transfers between devices with their start and end apart: 5 -> 8, of which waited for: 3 -> 6; matrix products, arithmetic and copies ran while one was open for 2% -> 3% of each run, Pallas kernels for 0% -> 40%
where the time goes in v1:
time: 145 us; the launch traced here: 144 us
  Pallas kernels  81 us (56%)
  starting transfers between devices  28.8 us (20%)
  waiting for transfers between devices  23.3 us (16%)
  local copies, waits for them, and re-layouts  10.7 us (7%)
    pallas_call x2, Pallas kernels, attend_call(): pl.pallas_call(body, in_specs=[pl.BlockSpec(memory_space=pltpu.SMEM)] + [...  34 us
    pallas_call x2, Pallas kernels, conv_call(): pl.pallas_call(body, grid=(hidden // CHUNK,), in_specs=[pl.BlockSpec(memo...  32.9 us
    all_to_all x4, waiting for transfers between devices, exchange(): lax.all_to_all(message, ('ha', 'wa'), split_axis=0, concat_axis=0, tiled=...  21.5 us
    all_to_all x4, starting transfers between devices, exchange(): lax.all_to_all(message, ('ha', 'wa'), split_axis=0, concat_axis=0, tiled=...  16.4 us
    pallas_call x2, Pallas kernels, mlp_call(): pl.pallas_call(body, grid=(1,), in_specs=specs, out_specs=pl.BlockSpec((1...  14.1 us
    unnamed x30, local copies, waits for them, and re-layouts  5.58 us
    ppermute x1, starting transfers between devices, body(): left = lax.ppermute(frames[:, :, cols - 1], 'wa', right_way)  4.79 us
    ppermute x1, starting transfers between devices, body(): top = lax.ppermute(edge(rows - 1), 'ha', down_way)  3.45 us
  transfers between devices with their start and end apart: 8, of which 6 were waited for; matrix products, arithmetic and copies ran while one was open for 3% of the time, Pallas kernels for 40%

profile of v1, /device:TPU:1, one launch (start us, length us, event | category | flops | bytes accessed | tf_op | source)
XLA Modules:
  0.0 144.3 jit_solution(14362129505521660962)
XLA Ops:
  0.0 1.1 fusion
  1.1 1.3 collective-permute-start.1
  2.4 0.0 copy-start.12
  2.4 0.0 copy-start.11
  2.5 4.8 %collective-permute-start = (bf16[2,16,384]{2,1,0:T(8,128)(2,1)S(1)}, bf16[2,16,384]{2,1,0:T(8,128)(2,1)S(1)}, u32[]{:S(2)}, u32[]{:S(2)}) collective-permute-start(bf16[2,16,384]{2,1,0:T(8,128)(2,1)S(1)} %bitcast.53), channel_id=1, source_target_pairs={{0,1},{1,2},{2,3},{4,5},{5,6},{6,7},{8,9},{9,10},{10,11},{12,13},{... | collective-permute-start | bytes 73736 | tf_op jit(solution)/shard_map/ppermute | solution.py:346
  7.3 1.5 %slice_bitcast_fusion = (bf16[16,64,384]{2,1,0:T(8,128)(2,1)S(1)}, bf16[16,64,384]{2,1,0:T(8,128)(2,1)S(1)}) fusion(bf16[2,16,64,384]{3,2,1,0:T(8,128)(2,1)} %param.13), kind=kLoop, calls=%fused_computation | loop fusion | bytes 3145728 | tf_op jit(solution)/shard_map/squeeze | solution.py:379
  8.8 0.0 copy-start
  8.8 0.0 copy-start.7
  8.8 0.0 copy-start.9
  8.8 0.0 copy-start.10
  8.8 1.1 slice_bitcast_fusion.2
  9.9 0.0 copy-done.12
  9.9 0.0 copy-done.11
  10.0 0.1 pad.7.clone
  10.1 0.0 collective-permute-done.1
  10.1 0.0 collective-permute-done
  10.1 0.1 maximum_maximum_fusion.1
  10.2 2.9 %collective-permute-start.3 = (bf16[2,80,384]{2,1,0:T(8,128)(2,1)S(1)}, bf16[2,80,384]{2,1,0:T(8,128)(2,1)S(1)}, u32[]{:S(2)}, u32[]{:S(2)}) collective-permute-start(bf16[2,80,384]{2,1,0:T(8,128)(2,1)S(1)} %get-tuple-element.26), channel_id=1, source_target_pairs={{4,0},{8,4},{12,8},{16,12},{20,16},{24,20},{28,24},{5,1},{9,5},{13... | collective-permute-start | bytes 368648 | tf_op jit(solution)/shard_map/ppermute | solution.py:356
  13.1 3.5 %collective-permute-start.2 = (bf16[2,80,384]{2,1,0:T(8,128)(2,1)S(1)}, bf16[2,80,384]{2,1,0:T(8,128)(2,1)S(1)}, u32[]{:S(2)}, u32[]{:S(2)}) collective-permute-start(bf16[2,80,384]{2,1,0:T(8,128)(2,1)S(1)} %get-tuple-element.27), channel_id=1, source_target_pairs={{0,4},{4,8},{8,12},{12,16},{16,20},{20,24},{24,28},{1,5},{5,9},{9,... | collective-permute-start | bytes 368648 | tf_op jit(solution)/shard_map/ppermute | solution.py:355
  16.6 0.6 collective-permute-done.3
  17.2 1.2 collective-permute-done.2
  18.4 0.0 copy-done
  18.4 0.0 copy-done.7
  18.4 0.0 copy-done.9
  18.5 0.0 copy-done.10
  18.5 0.0 copy-start.1
  18.5 1.3 copy-done.1
  19.7 16.5 %shard_map.129 = bf16[1024,384]{1,0:T(8,128)(2,1)} custom-call(s32[2,3]{1,0:T(2,128)S(1)} %copy-done.7, bf16[16,64,384]{2,1,0:T(8,128)(2,1)S(1)} %get-tuple-element.5.refs_1_, bf16[80,384]{1,0:T(8,128)(2,1)S(1)} %get-tuple-element.16.refs_2_, bf16[80,384]{1,0:T(8,128)(2,1)S(1)} %get-tuple-element.14.refs_3_, bf16[16,384]{1,0:T(8,128)(2,1)S(1)} %get-tuple-element.20.refs_4_, ...), custom_call_target="tpu_custom_call" | custom-call | flops 6000000000 | bytes 4000000 | tf_op jit(solution)/shard_map/pallas_call | solution.py:182
  36.2 6.4 %all-to-all-start.2 = ((bf16[32,32,384]{2,1,0:T(8,128)(2,1)}), bf16[32,32,384]{2,1,0:T(8,128)(2,1)S(1)}, u32[]{:S(2)}, u32[]{:S(2)}) async-start(bf16[32,32,384]{2,1,0:T(8,128)(2,1)} %bitcast.20), calls=%async_computation.2 | async-start | bytes 1572864 | tf_op jit(solution)/shard_map/all_to_all | solution.py:372
  42.6 0.0 copy-start.2
  42.6 1.3 copy-done.2
  43.8 16.5 %shard_map.127 = bf16[1024,384]{1,0:T(8,128)(2,1)} custom-call(s32[2,3]{1,0:T(2,128)S(1)} %copy-done.7, bf16[16,64,384]{2,1,0:T(8,128)(2,1)S(1)} %get-tuple-element.6.refs_1_, bf16[80,384]{1,0:T(8,128)(2,1)S(1)} %get-tuple-element.17.refs_2_, bf16[80,384]{1,0:T(8,128)(2,1)S(1)} %get-tuple-element.15.refs_3_, bf16[16,384]{1,0:T(8,128)(2,1)S(1)} %get-tuple-element.21.refs_4_, ...), custom_call_target="tpu_custom_call" | custom-call | flops 6000000000 | bytes 4000000 | tf_op jit(solution)/shard_map/pallas_call | solution.py:182
  60.3 3.1 %all-to-all-done.2 = bf16[32,32,384]{2,1,0:T(8,128)(2,1)S(1)} async-done(((bf16[32,32,384]{2,1,0:T(8,128)(2,1)}), bf16[32,32,384]{2,1,0:T(8,128)(2,1)S(1)}, u32[]{:S(2)}, u32[]{:S(2)}) %all-to-all-start.2) | async-done | bytes 786464 | tf_op jit(solution)/shard_map/all_to_all | solution.py:372
  63.4 3.2 %all-to-all-start = ((bf16[32,32,384]{2,1,0:T(8,128)(2,1)}), bf16[32,32,384]{2,1,0:T(8,128)(2,1)S(1)}, u32[]{:S(2)}, u32[]{:S(2)}) async-start(bf16[32,32,384]{2,1,0:T(8,128)(2,1)} %bitcast.9), calls=%async_computation | async-start | bytes 1572864 | tf_op jit(solution)/shard_map/all_to_all | solution.py:372
  66.6 0.0 copy-start.6
  66.6 1.3 fusion.1
  67.9 0.2 copy.26
  68.1 0.2 copy.25
  68.3 0.0 copy-done.6
  68.3 17.0 %shard_map.130 = bf16[1024,384]{1,0:T(8,128)(2,1)} custom-call(s32[2,3]{1,0:T(2,128)S(1)} %copy-done.7, bf16[1024,384]{1,0:T(8,128)(2,1)S(1)} %bitcast.44, bf16[384,384]{1,0:T(8,128)(2,1)S(1)} %bitcast.50, bf16[384,384]{1,0:T(8,128)(2,1)S(1)} %get-tuple-element.13.refs_3_, bf16[384,384]{1,0:T(8,128)(2,1)S(1)} %bitcast.48, bf16[384,384]{1,0:T(8,128)(2,1)S(1)} %copy-done.6), custom_call_target="tpu_custom_call" | custom-call | flops 6000000000 | bytes 3000000 | tf_op jit(solution)/shard_map/pallas_call | solution.py:263
  85.3 2.1 %all-to-all-done = bf16[32,32,384]{2,1,0:T(8,128)(2,1)S(1)} async-done(((bf16[32,32,384]{2,1,0:T(8,128)(2,1)}), bf16[32,32,384]{2,1,0:T(8,128)(2,1)S(1)}, u32[]{:S(2)}, u32[]{:S(2)}) %all-to-all-start) | async-done | bytes 786464 | tf_op jit(solution)/shard_map/all_to_all | solution.py:372
  87.4 3.8 %all-to-all-start.3 = ((bf16[32,32,384]{2,1,0:T(8,128)(2,1)}), bf16[32,32,384]{2,1,0:T(8,128)(2,1)S(1)}, u32[]{:S(2)}, u32[]{:S(2)}) async-start(bf16[32,32,384]{2,1,0:T(8,128)(2,1)} %bitcast.22), calls=%async_computation.3 | async-start | bytes 1572864 | tf_op jit(solution)/shard_map/all_to_all | solution.py:372
  91.2 17.0 %shard_map.128 = bf16[1024,384]{1,0:T(8,128)(2,1)} custom-call(s32[2,3]{1,0:T(2,128)S(1)} %copy-done.7, bf16[1024,384]{1,0:T(8,128)(2,1)S(1)} %bitcast.45, bf16[384,384]{1,0:T(8,128)(2,1)S(1)} %bitcast.51, bf16[384,384]{1,0:T(8,128)(2,1)S(1)} %get-tuple-element.13.refs_3_, bf16[384,384]{1,0:T(8,128)(2,1)S(1)} %bitcast.49, bf16[384,384]{1,0:T(8,128)(2,1)S(1)} %copy-done.6), custom_call_target="tpu_custom_call" | custom-call | flops 6000000000 | bytes 3000000 | tf_op jit(solution)/shard_map/pallas_call | solution.py:263
  108.1 0.0 copy-start.3
  108.1 0.0 copy-start.8
  108.2 3.8 %all-to-all-done.3 = bf16[32,32,384]{2,1,0:T(8,128)(2,1)S(1)} async-done(((bf16[32,32,384]{2,1,0:T(8,128)(2,1)}), bf16[32,32,384]{2,1,0:T(8,128)(2,1)S(1)}, u32[]{:S(2)}, u32[]{:S(2)}) %all-to-all-start.3) | async-done | bytes 786464 | tf_op jit(solution)/shard_map/all_to_all | solution.py:372
  112.0 3.2 %all-to-all-start.1 = ((bf16[32,32,384]{2,1,0:T(8,128)(2,1)}), bf16[32,32,384]{2,1,0:T(8,128)(2,1)S(1)}, u32[]{:S(2)}, u32[]{:S(2)}) async-start(bf16[32,32,384]{2,1,0:T(8,128)(2,1)} %bitcast.13), calls=%async_computation.1 | async-start | bytes 1572864 | tf_op jit(solution)/shard_map/all_to_all | solution.py:372
  115.2 0.0 copy-done.3
  115.2 0.0 copy-done.8
  115.2 0.0 copy-start.4
  115.2 1.3 copy-done.4
  116.4 7.0 %shard_map.131.refs_5_ = bf16[2,16,64,384]{3,2,1,0:T(8,128)(2,1)} custom-call(s32[2,3]{1,0:T(2,128)S(1)} %copy-done.7, bf16[1024,384]{1,0:T(8,128)(2,1)S(1)} %bitcast.46, bf16[128,128]{1,0:T(8,128)(2,1)S(1)} %copy-done.8, bf16[384,1536]{1,0:T(8,128)(2,1)S(1)} %copy-done.3, bf16[1536,384]{1,0:T(8,128)(2,1)S(1)} %copy-done.4), custom_call_target="tpu_custom_call" | custom-call | flops 5000000000 | bytes 4000000 | tf_op jit(solution)/shard_map/pallas_call | solution.py:308
  123.5 12.5 %all-to-all-done.1 = bf16[32,32,384]{2,1,0:T(8,128)(2,1)S(1)} async-done(((bf16[32,32,384]{2,1,0:T(8,128)(2,1)}), bf16[32,32,384]{2,1,0:T(8,128)(2,1)S(1)}, u32[]{:S(2)}, u32[]{:S(2)}) %all-to-all-start.1) | async-done | bytes 786464 | tf_op jit(solution)/shard_map/all_to_all | solution.py:372
  136.0 0.0 copy-start.5
  136.0 1.3 copy-done.5
  137.2 7.0 %shard_map.132 = bf16[2,16,64,384]{3,2,1,0:T(8,128)(2,1)} custom-call(s32[2,3]{1,0:T(2,128)S(1)} %copy-done.7, bf16[1024,384]{1,0:T(8,128)(2,1)S(1)} %bitcast.47, bf16[128,128]{1,0:T(8,128)(2,1)S(1)} %copy-done.8, bf16[384,1536]{1,0:T(8,128)(2,1)S(1)} %copy-done.3, bf16[1536,384]{1,0:T(8,128)(2,1)S(1)} %copy-done.5, ...), custom_call_target="tpu_custom_call", output_to_operand_aliasing={{}: (5, {})} | custom-call | flops 5000000000 | bytes 4000000 | tf_op jit(solution)/shard_map/pallas_call | solution.py:308
  (11 shorter events, 0.1 us)
Async XLA Ops:
  1.1 8.9 %collective-permute-start.1 = (bf16[2,16,384]{2,1,0:T(8,128)(2,1)S(1)}, bf16[2,16,384]{2,1,0:T(8,128)(2,1)S(1)}, u32[]{:S(2)}, u32[]{:S(2)}) collective-permute-start(bf16[2,16,384]{2,1,0:T(8,128)(2,1)S(1)} %bitcast.52), channel_id=1, source_target_pairs={{1,0},{2,1},{3,2},{5,4},{6,5},{7,6},{9,8},{10,9},{11,10},{13,12},{... | collective-permute-start | bytes 73736 | tf_op jit(solution)/shard_map/ppermute | solution.py:347
  2.4 7.5 %copy-start.12 = (f32[1536]{0:T(1024)S(1)}, f32[1536]{0:T(1024)}, u32[]{:S(2)}) copy-start(f32[1536]{0:T(1024)} %param.17) | copy-start | bytes 18436
  2.4 7.5 %copy-start.11 = (f32[3,3,1536]{2,1,0:T(4,128)S(1)}, f32[3,3,1536]{2,1,0:T(4,128)}, u32[]{:S(2)}) copy-start(f32[3,3,1536]{2,1,0:T(4,128)} %param.16) | copy-start | bytes 165892
  2.5 7.6 %collective-permute-start = (bf16[2,16,384]{2,1,0:T(8,128)(2,1)S(1)}, bf16[2,16,384]{2,1,0:T(8,128)(2,1)S(1)}, u32[]{:S(2)}, u32[]{:S(2)}) collective-permute-start(bf16[2,16,384]{2,1,0:T(8,128)(2,1)S(1)} %bitcast.53), channel_id=1, source_target_pairs={{0,1},{1,2},{2,3},{4,5},{5,6},{6,7},{8,9},{9,10},{10,11},{12,13},{... | collective-permute-start | bytes 73736 | tf_op jit(solution)/shard_map/ppermute | solution.py:346
  8.8 9.6 %copy-start = (bf16[384,1536]{1,0:T(8,128)(2,1)S(1)}, bf16[384,1536]{1,0:T(8,128)(2,1)}, u32[]{:S(2)}) copy-start(bf16[384,1536]{1,0:T(8,128)(2,1)} %refs_8_.3) | copy-start | bytes 3538948
  8.8 9.6 %copy-start.7 = (s32[2,3]{1,0:T(2,128)S(1)}, s32[2,3]{1,0:T(2,128)}, u32[]{:S(2)}) copy-start(s32[2,3]{1,0:T(2,128)} %refs_0_.11) | copy-start | bytes 76
  8.8 9.6 %copy-start.9 = (bf16[128,128]{1,0:T(8,128)(2,1)S(1)}, bf16[128,128]{1,0:T(8,128)(2,1)}, u32[]{:S(2)}) copy-start(bf16[128,128]{1,0:T(8,128)(2,1)} %constant.9.clone.refs_7_) | copy-start | bytes 98308
  8.8 9.6 %copy-start.10 = (bf16[128,128]{1,0:T(8,128)(2,1)S(1)}, bf16[128,128]{1,0:T(8,128)(2,1)}, u32[]{:S(2)}) copy-start(bf16[128,128]{1,0:T(8,128)(2,1)} %constant.8.clone.refs_6_) | copy-start | bytes 98308
  10.2 7.0 %collective-permute-start.3 = (bf16[2,80,384]{2,1,0:T(8,128)(2,1)S(1)}, bf16[2,80,384]{2,1,0:T(8,128)(2,1)S(1)}, u32[]{:S(2)}, u32[]{:S(2)}) collective-permute-start(bf16[2,80,384]{2,1,0:T(8,128)(2,1)S(1)} %get-tuple-element.26), channel_id=1, source_target_pairs={{4,0},{8,4},{12,8},{16,12},{20,16},{24,20},{28,24},{5,1},{9,5},{13... | collective-permute-start | bytes 368648 | tf_op jit(solution)/shard_map/ppermute | solution.py:356
  13.1 5.3 %collective-permute-start.2 = (bf16[2,80,384]{2,1,0:T(8,128)(2,1)S(1)}, bf16[2,80,384]{2,1,0:T(8,128)(2,1)S(1)}, u32[]{:S(2)}, u32[]{:S(2)}) collective-permute-start(bf16[2,80,384]{2,1,0:T(8,128)(2,1)S(1)} %get-tuple-element.27), channel_id=1, source_target_pairs={{0,4},{4,8},{8,12},{12,16},{16,20},{20,24},{24,28},{1,5},{5,9},{9,... | collective-permute-start | bytes 368648 | tf_op jit(solution)/shard_map/ppermute | solution.py:355
  18.5 1.3 copy-start.1
  36.2 27.2 %all-to-all-start.2 = ((bf16[32,32,384]{2,1,0:T(8,128)(2,1)}), bf16[32,32,384]{2,1,0:T(8,128)(2,1)S(1)}, u32[]{:S(2)}, u32[]{:S(2)}) async-start(bf16[32,32,384]{2,1,0:T(8,128)(2,1)} %bitcast.20), calls=%async_computation.2 | async-start | bytes 1572864 | tf_op jit(solution)/shard_map/all_to_all | solution.py:372
  42.6 1.3 copy-start.2
  63.4 24.0 %all-to-all-start = ((bf16[32,32,384]{2,1,0:T(8,128)(2,1)}), bf16[32,32,384]{2,1,0:T(8,128)(2,1)S(1)}, u32[]{:S(2)}, u32[]{:S(2)}) async-start(bf16[32,32,384]{2,1,0:T(8,128)(2,1)} %bitcast.9), calls=%async_computation | async-start | bytes 1572864 | tf_op jit(solution)/shard_map/all_to_all | solution.py:372
  66.6 1.7 %copy-start.6 = (bf16[384,384]{1,0:T(8,128)(2,1)S(1)}, bf16[384,384]{1,0:T(8,128)(2,1)}, u32[]{:S(2)}) copy-start(bf16[384,384]{1,0:T(8,128)(2,1)} %refs_5_.3) | copy-start | bytes 884740
  87.4 24.6 %all-to-all-start.3 = ((bf16[32,32,384]{2,1,0:T(8,128)(2,1)}), bf16[32,32,384]{2,1,0:T(8,128)(2,1)S(1)}, u32[]{:S(2)}, u32[]{:S(2)}) async-start(bf16[32,32,384]{2,1,0:T(8,128)(2,1)} %bitcast.22), calls=%async_computation.3 | async-start | bytes 1572864 | tf_op jit(solution)/shard_map/all_to_all | solution.py:372
  108.1 7.0 %copy-start.3 = (bf16[384,1536]{1,0:T(8,128)(2,1)S(1)}, bf16[384,1536]{1,0:T(8,128)(2,1)}, u32[]{:S(2)}) copy-start(bf16[384,1536]{1,0:T(8,128)(2,1)} %refs_3_.3) | copy-start | bytes 3538948
  108.1 7.0 %copy-start.8 = (bf16[128,128]{1,0:T(8,128)(2,1)S(1)}, bf16[128,128]{1,0:T(8,128)(2,1)}, u32[]{:S(2)}) copy-start(bf16[128,128]{1,0:T(8,128)(2,1)} %constant.10.clone.refs_2_) | copy-start | bytes 98308
  112.0 24.0 %all-to-all-start.1 = ((bf16[32,32,384]{2,1,0:T(8,128)(2,1)}), bf16[32,32,384]{2,1,0:T(8,128)(2,1)S(1)}, u32[]{:S(2)}, u32[]{:S(2)}) async-start(bf16[32,32,384]{2,1,0:T(8,128)(2,1)} %bitcast.13), calls=%async_computation.1 | async-start | bytes 1572864 | tf_op jit(solution)/shard_map/all_to_all | solution.py:372
  115.2 1.3 copy-start.4
  136.0 1.3 copy-start.5
